TPU v7x, 512 devices: a whole 4x8x8 slice. The times are simulated.
512 devices in a mesh: fsdp: 16 (over x, y_lo, core), seq: 32 (over z, y_hi).
Axes of the slice: x: 4, y: 8 (y_hi: 4, y_lo: 2; y = y_hi * 2 + y_lo), z: 8, core: 2. Of those that a mesh axis runs over, the one named last changes fastest.
Arguments:
- conv_input: bfloat16 [16, 4096, 5120], P('fsdp', 'seq'), may hold values from -6 to 6
- gate_input: bfloat16 [16, 4096, 4096], P('fsdp', 'seq'), may hold values from -6 to 6
- step_input: bfloat16 [16, 4096, 64], P('fsdp', 'seq'), may hold values from -3 to 3
- conv_weight: float32 [4, 5120], P(None, 'fsdp'), may hold values from -3 to 3
- conv_bias: float32 [5120], P('fsdp'), may hold values from -3 to 3
- decay_log: float32 [64], P('fsdp'), may hold values from -2.1 to 1.7
- step_bias: float32 [64], P('fsdp'), may hold values from -13 to -3.7
- skip_weight: float32 [64], P('fsdp'), may hold values from 0.5 to 2
- norm_gain: float32 [4096], P('fsdp'), may hold values from 0.5 to 1.5
Outputs:
- mixer_out: bfloat16 [16, 4096, 4096], P('fsdp', 'seq')
All inputs are finite; a program needn't handle non-finite values.
Results may differ from a plain program's by a relative error of at most 0.0045.
Values may be sent and summed in bfloat16 or wider, within the bound.
A program may use at most 192 MiB of HBM per device.

v0:
```python
import jax
import jax.numpy as jnp
from jax import lax
from jax.sharding import PartitionSpec as P

HEADS = 64
HEAD_DIM = 64
STATE = 128
GROUPS = 4
KERNEL = 4
BLOCK = 128
INNER = 4096
CONV_DIM = 5120


HIGH = lax.Precision.HIGHEST
EPS = 1e-05


def shifted(block, axis, distance):
    devices = range(lax.axis_size(axis))
    route = [(i - distance, i) for i in devices if i - distance in devices]
    return lax.ppermute(block, axis, route)


def prefix(part, axis, combine, identity):
    place = lax.axis_index(axis)
    gathered = jax.tree.map(lambda a: lax.all_gather(a, axis), part)
    state = jax.tree.map(lambda a, e: jnp.zeros_like(a) + jnp.asarray(e, a.dtype), part, identity)

    def one(lap, state):
        return combine(
            state, jax.tree.map(lambda a: lax.dynamic_index_in_dim(a, lap, 0, False), gathered)
        )

    return lax.fori_loop(0, place, one, state)


def mix_inputs(padded_rows, conv_weight, conv_bias, step_rows, step_bias, decay_log):
    length = padded_rows.shape[0] - (KERNEL - 1)
    summed = conv_bias[None, :] + jnp.zeros((length, CONV_DIM), jnp.float32)
    for offset in range(KERNEL):
        summed = summed + conv_weight[offset][None, :] * padded_rows[offset : offset + length]
    activated = jax.nn.silu(summed)
    input_flat = activated[:, :INNER]
    key_flat = activated[:, INNER : INNER + GROUPS * STATE]
    query_flat = activated[:, INNER + GROUPS * STATE :]
    dt_step = jax.nn.softplus(step_rows.astype(jnp.float32) + step_bias[None, :])
    return (input_flat, key_flat, query_flat, dt_step, -jnp.exp(decay_log))


def run_block(memory, in_block, key_block, query_block, step_block, rate_coef):
    length = in_block.shape[2]
    per_group = HEADS // GROUPS
    cumul = jnp.cumsum(step_block * rate_coef[:, None], axis=1)
    positions = jnp.arange(length)
    causal = (positions[:, None] >= positions[None, :])[None, :, :]
    spread = jnp.where(causal, cumul[:, :, None] - cumul[:, None, :], 0.0)
    decays = jnp.where(causal, jnp.exp(spread), 0.0)
    scores = jnp.einsum("gtn,gsn->gts", query_block, key_block, precision=HIGH)
    weights = (
        decays.reshape(GROUPS, per_group, length, length)
        * scores[:, None, :, :]
        * step_block.reshape(GROUPS, per_group, 1, length)
    )
    input_groups = in_block.reshape(GROUPS, per_group, HEAD_DIM, length)
    inside = jnp.einsum("gkts,gkps->gkpt", weights, input_groups, precision=HIGH).reshape(
        HEADS, HEAD_DIM, length
    )
    carried = jnp.einsum(
        "gtn,gmn->gmt",
        query_block,
        memory.reshape(GROUPS, per_group * HEAD_DIM, STATE),
        precision=HIGH,
    )
    inside = inside + jnp.exp(cumul)[:, None, :] * carried.reshape(HEADS, HEAD_DIM, length)
    remaining = (jnp.exp(cumul[:, -1:] - cumul) * step_block).reshape(GROUPS, per_group, 1, length)
    update = jnp.einsum("gkps,gsn->gkpn", input_groups * remaining, key_block, precision=HIGH)
    new_memory = (
        update.reshape(HEADS, HEAD_DIM, STATE) + jnp.exp(cumul[:, -1])[:, None, None] * memory
    )
    return (new_memory, inside)


def stack_blocks(input_flat, key_flat, query_flat, dt_step):
    count = input_flat.shape[0] // BLOCK
    return (
        input_flat.reshape(count, BLOCK, HEADS, HEAD_DIM).transpose(0, 2, 3, 1),
        key_flat.reshape(count, BLOCK, GROUPS, STATE).transpose(0, 2, 1, 3),
        query_flat.reshape(count, BLOCK, GROUPS, STATE).transpose(0, 2, 1, 3),
        dt_step.reshape(count, BLOCK, HEADS).transpose(0, 2, 1),
    )


def gated_norm(values, gate_rows, norm_gain):
    length = values.shape[0]
    gated_rows = values * jax.nn.silu(gate_rows.astype(jnp.float32))
    grouped = gated_rows.reshape(length, GROUPS, INNER // GROUPS)
    inverse_rms = lax.rsqrt(jnp.mean(grouped * grouped, axis=2, keepdims=True) + EPS)
    return ((grouped * inverse_rms).reshape(length, INNER) * norm_gain[None, :]).astype(
        jnp.bfloat16
    )


def combine_pairs(first, second):
    return (first[0] * second[0], second[0][:, None, None] * first[1] + second[1])


def body(
    conv_input,
    gate_input,
    step_input,
    conv_weight,
    conv_bias,
    decay_log,
    step_bias,
    skip_weight,
    norm_gain,
):
    conv_weight, conv_bias, decay_log, step_bias, skip_weight, norm_gain = (
        lax.all_gather(conv_weight, "fsdp", axis=1, tiled=True),
        lax.all_gather(conv_bias, "fsdp", axis=0, tiled=True),
        lax.all_gather(decay_log, "fsdp", axis=0, tiled=True),
        lax.all_gather(step_bias, "fsdp", axis=0, tiled=True),
        lax.all_gather(skip_weight, "fsdp", axis=0, tiled=True),
        lax.all_gather(norm_gain, "fsdp", axis=0, tiled=True),
    )
    length = conv_input.shape[1]
    earlier = shifted(conv_input[:, length - (KERNEL - 1) :, :], "seq", 1)
    padded_rows = jnp.concatenate([earlier, conv_input], 1)[0].astype(jnp.float32)
    input_flat, key_flat, query_flat, dt_step, rate_coef = mix_inputs(
        padded_rows, conv_weight, conv_bias, step_input[0], step_bias, decay_log
    )

    def advance(memory, pieces):
        return run_block(memory, pieces[0], pieces[1], pieces[2], pieces[3], rate_coef)

    stacked = stack_blocks(input_flat, key_flat, query_flat, dt_step)
    local_memory, outputs = lax.scan(
        advance, jnp.zeros((HEADS, HEAD_DIM, STATE), jnp.float32), stacked
    )
    cumul = jnp.cumsum(dt_step * rate_coef[None, :], axis=0)
    through = jnp.exp(cumul[-1])
    _, incoming = prefix(
        (through, local_memory),
        "seq",
        combine_pairs,
        (jnp.ones_like(through), jnp.zeros_like(local_memory)),
    )
    per_group = HEADS // GROUPS
    query_groups = query_flat.reshape(length, GROUPS, STATE).transpose(1, 0, 2)
    carried = jnp.einsum(
        "gtn,gmn->gtm",
        query_groups,
        incoming.reshape(GROUPS, per_group * HEAD_DIM, STATE),
        precision=HIGH,
    )
    carried = carried.transpose(1, 0, 2).reshape(length, INNER) * jnp.repeat(
        jnp.exp(cumul), HEAD_DIM, axis=1
    )
    local_values = outputs.transpose(0, 3, 1, 2).reshape(length, INNER)
    values = local_values + carried + jnp.repeat(skip_weight, HEAD_DIM)[None, :] * input_flat
    return gated_norm(values, gate_input[0], norm_gain)[None]


def solution(mesh):
    return jax.shard_map(
        body,
        mesh=mesh,
        in_specs=(
            P("fsdp", "seq", None),
            P("fsdp", "seq", None),
            P("fsdp", "seq", None),
            P(None, "fsdp"),
            P("fsdp"),
            P("fsdp"),
            P("fsdp"),
            P("fsdp"),
            P("fsdp"),
        ),
        out_specs=P("fsdp", "seq", None),
        check_vma=False,
    )
```

profile of v0, /device:TPU:504, one launch (start us, length us, event | category | flops | bytes accessed | tf_op | source)
XLA Modules:
  0.0 905.6 jit_solution(1385661165451511118)
XLA Ops:
  11.3 17.9 %all-gather = f32[16,320,4]{1,2,0:T(4,128)S(1)} all-gather(f32[1,320,4]{1,2,0:T(4,128)} %bitcast.186), channel_id=1, replica_groups=mesh['fsdp'=16,'seq'=32] {'fsdp'}, dimensions={0}, use_global_device_ids=true | all-gather | bytes 87040 | tf_op jit(solution)/shard_map/all_gather | solution.py:121
  32.8 51.6 %all-reduce.4 = (f32[5120]{0:T(1024)S(1)}, f32[64]{0:T(128)S(1)}, f32[64]{0:T(128)S(1)}, f32[64]{0:T(128)S(1)}) all-reduce(f32[5120]{0:T(1024)S(1)} %dynamic-update-slice, f32[64]{0:T(128)S(1)} %dynamic-update-slice.1, f32[64]{0:T(128)S(1)} %dynamic-update-slice.2, f32[64]{0:T(128)S(1)} %dynamic-update-slice.3), channel_id=1, replica_groups=mesh['fsdp'=16,'seq'=32] {'fsdp'}, use_global_device_ids=true, to_apply=%add | all-reduce | flops 5312 | bytes 42496
  90.1 6.4 divide_multiply_fusion
  98.2 2.0 fusion.22
  103.0 2.3 copy.33
  105.3 87.7 %all-gather.1 = f32[32,1,64]{2,1,0:T(1,128)S(1)} all-gather(f32[1,1,64]{2,1,0:T(1,128)S(1)} %fusion.53), channel_id=1, replica_groups=mesh['fsdp'=16,'seq'=32] {'seq'}, dimensions={0}, use_global_device_ids=true | all-gather | bytes 8448 | tf_op jit(solution)/shard_map/all_gather | solution.py:28
  193.0 15.5 %all-gather.2 = f32[16,1,256]{2,1,0:T(1,128)S(1)} all-gather(f32[1,1,256]{2,1,0:T(1,128)S(1)} %bitcast.187), channel_id=1, replica_groups=mesh['fsdp'=16,'seq'=32] {'fsdp'}, dimensions={0}, use_global_device_ids=true | all-gather | bytes 17408 | tf_op jit(solution)/shard_map/all_gather | solution.py:126
  211.3 8.4 fusion
  221.6 602.6 %all-gather.5.cloned.1.call-done = f32[32,64,64,128]{3,2,1,0:T(8,128)} async-done(((f32[1,64,64,128]{3,2,1,0:T(8,128)}), f32[32,64,64,128]{3,2,1,0:T(8,128)}) %all-gather.5.cloned.1.call-update) | async-done | bytes 67108880 | tf_op jit(solution)/shard_map/all_gather | solution.py:28
  824.5 63.0 %while.3 = (s32[]{:T(128)}, f32[64,64,128]{2,1,0:T(8,128)S(1)}, s32[]{:T(128)}, f32[32,64]{1,0:T(8,128)S(1)}, f32[32,64,64,128]{3,2,1,0:T(8,128)}, /*index=5*/s32[]{:T(128)}, s32[]{:T(128)}, s32[]{:T(128)}) while((s32[]{:T(128)}, f32[64,64,128]{2,1,0:T(8,128)S(1)}, s32[]{:T(128)}, f32[32,64]{1,0:T(8,128)S(1)}, f32[32,64,64,128]{3,2,1,0:T(8,128)}, ...), condition=%wide.region_3.4_spmd, body=%wide.region_2.3_spmd.sunk | while | flops 1048581 | bytes 6292351 | solution.py:36
  824.5 2.0 bitcast_add_fusion.5
  826.5 2.0 bitcast_add_fusion.5
  828.5 2.0 bitcast_add_fusion.5
  830.6 2.0 bitcast_add_fusion.5
  832.6 2.0 bitcast_add_fusion.5
  834.6 2.0 bitcast_add_fusion.5
  838.7 2.0 bitcast_add_fusion.5
  840.7 2.0 bitcast_add_fusion.5
  842.7 2.0 bitcast_add_fusion.5
  848.8 2.0 bitcast_add_fusion.5
  850.8 2.0 bitcast_add_fusion.5
  858.9 2.0 bitcast_add_fusion.5
  860.9 2.0 bitcast_add_fusion.5
  867.0 2.0 bitcast_add_fusion.5
  869.0 2.0 bitcast_add_fusion.5
  871.0 2.0 bitcast_add_fusion.5
  877.1 2.0 bitcast_add_fusion.5
  879.1 2.0 bitcast_add_fusion.5
  881.2 2.0 bitcast_add_fusion.5
  887.4 3.2 convolution_bitcast_fusion
  890.6 3.1 copy.31
  893.7 3.0 bitcast_reduce_fusion
  (101 shorter events, 48.0 us)
Async XLA Ops:
  6.5 817.7 %all-gather.5.cloned.1.call-start = ((), (), s32[]{:S(2)}) async-start(), calls=%async_computation | async-start | bytes 69206016 | tf_op jit(solution)/shard_map/all_gather | solution.py:28
  7.5 81.0 %collective-permute-start = (bf16[1,3,5120]{2,1,0:T(4,128)(2,1)S(1)}, bf16[1,3,5120]{2,1,0:T(4,128)(2,1)S(1)}, u32[]{:S(2)}, u32[]{:S(2)}) collective-permute-start(bf16[1,3,5120]{2,1,0:T(4,128)(2,1)S(1)} %slice.57), channel_id=1, source_target_pairs={{0,1},{1,2},{2,3},{3,4},{4,5},{5,6},{6,7},{7,8},{8,9},{9,10},{10,1... | collective-permute-start | bytes 92168 | tf_op jit(solution)/shard_map/ppermute | solution.py:23
  96.5 1.5 copy-start
  101.7 0.7 copy-start.2
  101.7 91.3 %copy-start.3 = (f32[256]{0:T(256)S(1)}, f32[256]{0:T(256)}, u32[]{:S(2)}) copy-start(f32[256]{0:T(256)} %param.19) | copy-start | bytes 3076
  890.6 3.1 copy-start.1
Sparse Core Ops, SparseCore 0:
  101.9 722.2 all-gather.4
where the time goes:
time: 907 us; the launch traced here: 906 us
  waiting for transfers between devices  603 us (66%)
  blocking collectives  173 us (19%)
  other arithmetic  78.2 us (9%)
  local copies, waits for them, and re-layouts  18.3 us (2%)
  matrix products  16.1 us (2%)
  between operations  14.9 us (2%)
    all_gather x1, waiting for transfers between devices, prefix(): gathered = jax.tree.map(lambda a: lax.all_gather(a, axis), part)  603 us
    all_gather x1, blocking collectives, prefix(): gathered = jax.tree.map(lambda a: lax.all_gather(a, axis), part)  87.7 us
    add x31, other arithmetic, combine_pairs(): second[0][:, None, None] * first[1] + second[1]  61.2 us
    unnamed x1, blocking collectives  51.6 us
  transfers between devices with their start and end apart: 2, of which 1 were waited for; matrix products, arithmetic and copies ran while one was open for 3% of the time, Pallas kernels for 0%

commit v1 on v0

v1 whole, which is shorter than its diff:
```python
import functools

import jax
import jax.numpy as jnp
from jax import lax
from jax.experimental import pallas as pl
from jax.experimental.pallas import tpu as pltpu
from jax.sharding import PartitionSpec as P

HEADS = 64
GROUPS = 4
KERNEL = 4
INNER = 4096
CONV_DIM = 5120
EPS = 1e-05
ROWS = 128
LANES = 128
TILES = INNER // LANES
PER_GROUP = TILES // GROUPS
LOG2E = 1.4426950408889634
MESH = pl.DeviceIdType.MESH
F32 = jnp.float32
BF16 = jnp.bfloat16


def dot(a, b):
    return jnp.dot(a, b, preferred_element_type=F32)


def silu(v):
    half = 0.5 * v
    return half + half * jnp.tanh(half)


def three_parts(v):
    top = v.astype(BF16).astype(F32)
    rest = v - top
    middle = rest.astype(BF16).astype(F32)
    return top, middle, rest - middle


def remote(src, dst, send, recv, device):
    return pltpu.make_async_remote_copy(
        src_ref=src, dst_ref=dst, send_sem=send, recv_sem=recv,
        device_id=device, device_id_type=MESH,
    )


def kernel(
    ranks, shards,
    conv_hbm, gate_hbm, step_hbm, weight_ref, bias_ref, decay_ref, step_bias_ref, skip_ref, gain_ref,
    out_hbm,
    conv_v, gate_v, step_v, tail_v, halo_pack, halo_send, halo_recv, halo,
    par_send, par, wfull, gfull,
    wide, cparts, logdt, keyt, query, scores,
    xs, vals, expc, gates, square, out_v,
    local_send, local_recv, decay_send, decay_recv, state_send, state_recv,
    load_sem, out_sem, halo_sem, par_sem, loc_sem, dec_sem, st_send_sem, st_recv_sem,
):
    me = lax.axis_index("seq")
    shard = lax.axis_index("fsdp")

    def load(src, dst, slot):
        return pltpu.make_async_copy(src, dst, load_sem.at[slot])

    tail_load = load(conv_hbm.at[0, pl.ds(ROWS - 16, 16)], tail_v, 0)
    step_load = load(step_hbm.at[0], step_v, 1)
    conv_load = load(conv_hbm.at[0], conv_v, 2)
    gate_load = load(gate_hbm.at[0], gate_v, 3)
    tail_load.start()
    step_load.start()
    conv_load.start()
    gate_load.start()

    barrier = pltpu.get_barrier_semaphore()

    def greet_rank(k, c):
        pl.semaphore_signal(barrier, inc=1, device_id={"seq": lax.rem(me + k, ranks)}, device_id_type=MESH)
        return c

    def greet_shard(k, c):
        pl.semaphore_signal(barrier, inc=1, device_id={"fsdp": lax.rem(shard + k, shards)}, device_id_type=MESH)
        return c

    lax.fori_loop(1, shards, greet_shard, 0)
    lax.fori_loop(1, ranks, greet_rank, 0)

    width = CONV_DIM // shards
    heads = HEADS // shards
    par_send[...] = jnp.zeros_like(par_send)
    odd = lax.rem(shard, 2)

    @pl.when(odd == 0)
    def _():
        par_send[0:4, 0:width] = weight_ref[...]
        par_send[4:5, 0:width] = bias_ref[...].reshape(1, width)

    @pl.when(odd == 1)
    def _():
        par_send[0:4, 64 : 64 + width] = weight_ref[...]
        par_send[4:5, 64 : 64 + width] = bias_ref[...].reshape(1, width)

    par_send[5:6, 0:256] = gain_ref[...].reshape(1, 256)
    lane = lax.broadcasted_iota(jnp.int32, (1, LANES), 1)
    for place, ref in enumerate((decay_ref, step_bias_ref, skip_ref)):
        row = jnp.zeros((1, LANES), F32)
        for h in range(heads):
            row = jnp.where(lane == shard * heads + h, ref[h], row)
            row = jnp.where(lane == HEADS + shard * heads + h, ref[h], row)
        par_send[6:7, place * LANES : (place + 1) * LANES] = row

    tail_load.wait()
    halo_pack[15:16, :] = jnp.zeros((1, 1024), F32)
    tail = tail_v[...].astype(F32)
    for r in range(KERNEL - 1):
        for c in range(CONV_DIM // 1024):
            halo_pack[r * 5 + c : r * 5 + c + 1, :] = tail[13 + r : 14 + r, c * 1024 : (c + 1) * 1024]
    halo_send[...] = halo_pack[...].astype(BF16)

    pl.semaphore_wait(barrier, ranks + shards - 2)

    halo_copy = remote(halo_send, halo_recv, halo_sem.at[0], halo_sem.at[1], {"seq": lax.rem(me + 1, ranks)})
    halo_copy.start()

    def send_par(k, c):
        remote(par_send, par.at[shard], par_sem.at[0], par_sem.at[1],
               {"fsdp": lax.rem(shard + k, shards)}).start()
        return c

    lax.fori_loop(1, shards, send_par, 0)
    par[shard] = par_send[...]

    gate_load.wait()

    def gate_tile(o, c):
        at = pl.ds(pl.multiple_of(o * LANES, LANES), LANES)
        gates[o] = silu(gate_v[:, at].astype(F32)).astype(gates.dtype)
        return c

    lax.fori_loop(0, TILES, gate_tile, 0)
    conv_load.wait()
    step_load.wait()

    several = par.at[pl.ds(0, shards - 1)]
    pltpu.make_async_copy(several, several, par_sem.at[1]).wait()
    for j in range(shards // 2):
        left, right = par[2 * j], par[2 * j + 1]
        at = 5 * j * LANES
        wfull[:, at : at + 256] = left[:, 0:256]
        wfull[:, at + 256 : at + 384] = left[:, 256:384] + right[:, 0:128]
        wfull[:, at + 384 : at + 640] = right[:, 128:384]
    small = jnp.zeros((1, 3 * LANES), F32)
    for i in range(shards):
        gfull[:, i * 256 : (i + 1) * 256] = par[i, 5:6, 0:256]
        small = small + par[i, 6:7, :]
    decay_row, bias_row, skip_row = (small[:, i * LANES : (i + 1) * LANES] for i in range(3))

    halo_copy.wait()
    before = jnp.where(me == 0, 0.0, halo_recv[...].astype(F32))
    for r in range(KERNEL - 1):
        for c in range(CONV_DIM // 1024):
            halo[5 + r : 6 + r, c * 1024 : (c + 1) * 1024] = before[r * 5 + c : r * 5 + c + 1, :]

    def convolved(at):
        rows = jnp.concatenate([halo[:, at], conv_v[:, at].astype(F32)], axis=0)
        taps = wfull[:, at]
        total = taps[4:5] + taps[3:4] * rows[8:]
        for back in range(1, KERNEL):
            total = total + taps[3 - back : 4 - back] * pltpu.roll(rows, back, 0)[8:]
        return silu(total)

    step = step_v[...].astype(F32)
    step = jnp.concatenate([step, step], axis=0).T
    dt = jax.nn.softplus(step + bias_row)
    after = lax.broadcasted_iota(jnp.int32, (ROWS, ROWS), 0)
    ahead = lax.broadcasted_iota(jnp.int32, (ROWS, ROWS), 1)
    causal = after >= ahead
    lower = jnp.where(causal, 1.0, 0.0)
    rate2 = -jnp.exp(decay_row) * LOG2E
    cumul = jnp.dot(lower, dt * rate2, precision=lax.Precision.HIGHEST, preferred_element_type=F32)
    low_half = lax.broadcasted_iota(jnp.int32, (ROWS, LANES), 1) < HEADS

    def spread_parts(v):
        top, middle, low = three_parts(v)
        first = jnp.where(low_half[: v.shape[0]], top, middle)
        return first.astype(BF16), jnp.where(low_half[: v.shape[0]], low, 0.0).astype(BF16)

    cparts[:, 0:LANES], cparts[:, LANES:] = spread_parts(cumul)
    logdt[...] = jnp.log2(dt).T - cumul.T
    wide[0:ROWS, 0:LANES], wide[0:ROWS, LANES:] = spread_parts(dt * jnp.exp2(cumul[ROWS - 1 : ROWS] - cumul))
    wide[ROWS : 2 * ROWS, 0:LANES], wide[ROWS : 2 * ROWS, LANES:] = spread_parts(jnp.exp2(cumul))
    skip16 = jnp.broadcast_to(skip_row, (16, LANES))
    wide[2 * ROWS :, 0:LANES], wide[2 * ROWS :, LANES:] = spread_parts(skip16)

    for g in range(GROUPS):
        keys = convolved(slice(INNER + g * LANES, INNER + (g + 1) * LANES))
        keyt[g] = keys.T.astype(BF16)
        asked = convolved(slice(INNER + (GROUPS + g) * LANES, INNER + (GROUPS + g + 1) * LANES))
        query[g] = asked.astype(BF16)
        scores[g] = jnp.where(causal, dot(query[g], keyt[g]), 0.0)

    pick_row = lax.rem(lax.broadcasted_iota(jnp.int32, (2 * LANES, LANES), 0), HEADS)
    pick_half = lax.broadcasted_iota(jnp.int32, (2 * LANES, LANES), 1) // HEADS

    def local_state(o, state_ref, decay_out):
        at = pl.ds(pl.multiple_of(o * LANES, LANES), LANES)
        x = convolved(at)
        pick = jnp.where(pick_row == pick_half + 2 * o, 1.0, 0.0).astype(BF16)
        spread = dot(wide[...], pick)
        expc[o] = spread[ROWS : 2 * ROWS]
        xs[o] = x.astype(BF16)
        vals[o] = x * spread[2 * ROWS : 2 * ROWS + 1]
        weighted = (x * spread[0:ROWS]).astype(BF16)
        state_ref[...] = dot(keyt[o // PER_GROUP], weighted).astype(BF16)
        decay_out[...] = spread[2 * ROWS - 1 : 2 * ROWS]

    def first_pass(k, c):
        o = lax.rem(me + k, ranks)
        local_state(o, local_send.at[o], decay_send.at[o])
        remote(local_send.at[o], local_recv.at[me], loc_sem.at[0], loc_sem.at[1], {"seq": o}).start()
        remote(decay_send.at[o], decay_recv.at[me], dec_sem.at[0], dec_sem.at[1], {"seq": o}).start()
        return c

    lax.fori_loop(1, ranks, first_pass, 0)
    local_state(me, local_recv.at[me], decay_recv.at[me])

    ones_row = lax.rem(lax.broadcasted_iota(jnp.int32, (2 * LANES, 2 * LANES), 0), HEADS)
    ones_half = lax.broadcasted_iota(jnp.int32, (2 * LANES, 2 * LANES), 1) // LANES

    def inside(o, c):
        pick = jnp.where(ones_row == ones_half + 2 * o, 1.0, 0.0).astype(BF16)
        spread = dot(cparts[...], pick)
        score = scores[o // PER_GROUP]
        x = xs[o]
        zero = jnp.zeros_like(x)
        total = vals[o]
        for half in range(2):
            spot = spread[:, half * LANES : (half + 1) * LANES] + logdt[pl.ds(2 * o + half, 1), :]
            weights = jnp.exp2(jnp.minimum(spot, 64.0)) * score
            mine = jnp.where(low_half if half == 0 else jnp.logical_not(low_half), x, zero)
            total = total + dot(weights.astype(BF16), mine)
        vals[o] = total
        return c

    lax.fori_loop(0, TILES, inside, 0)

    most = local_recv.at[pl.ds(0, ranks - 1)]
    pltpu.make_async_copy(most, most, loc_sem.at[1]).wait()
    most_decay = decay_recv.at[pl.ds(0, ranks - 1)]
    pltpu.make_async_copy(most_decay, most_decay, dec_sem.at[1]).wait()

    def carry(s, state):
        state_send[s] = state.astype(BF16)
        return state * decay_recv[s] + local_recv[s].astype(F32)

    lax.fori_loop(0, ranks, carry, jnp.zeros((LANES, LANES), F32))

    def send_state(k, c):
        s = lax.rem(me + k, ranks)
        remote(state_send.at[s], state_recv.at[me], st_send_sem, st_recv_sem.at[me], {"seq": s}).start()
        return c

    lax.fori_loop(1, ranks, send_state, 0)
    square[...] = jnp.zeros_like(square)

    def finish(o, state):
        g = o // PER_GROUP
        value = (vals[o] + dot(query[g], state) * expc[o]) * gates[o].astype(F32)
        vals[o] = value
        square[g] = square[g] + value * value

    finish(me, state_send[me])

    def arrive(k, c):
        o = lax.rem(me + ranks - k, ranks)
        slot = state_recv.at[o]
        pltpu.make_async_copy(slot, slot, st_recv_sem.at[o]).wait()
        finish(o, state_recv[o])
        return c

    lax.fori_loop(1, ranks, arrive, 0)

    writes = []
    for g in range(GROUPS):
        mean = jnp.sum(square[g], axis=1, keepdims=True) * (1.0 / (PER_GROUP * LANES))
        inverse = lax.rsqrt(mean + EPS)
        for j in range(PER_GROUP):
            o = g * PER_GROUP + j
            out_v[:, o * LANES : (o + 1) * LANES] = (
                vals[o] * inverse * gfull[:, o * LANES : (o + 1) * LANES]
            ).astype(BF16)
        part = slice(g * 1024, (g + 1) * 1024)
        write = pltpu.make_async_copy(out_v.at[:, part], out_hbm.at[0, :, part], out_sem.at[g])
        write.start()
        writes.append(write)

    pltpu.make_async_copy(several, several, par_sem.at[0]).wait()
    pltpu.make_async_copy(most, most, loc_sem.at[0]).wait()
    pltpu.make_async_copy(most_decay, most_decay, dec_sem.at[0]).wait()
    sent = state_send.at[pl.ds(0, ranks - 1)]
    pltpu.make_async_copy(sent, sent, st_send_sem).wait()
    for write in writes:
        write.wait()


def mixer(ranks, shards, *operands):
    tile = (TILES, ROWS, LANES)
    pair = (ranks, LANES, LANES)
    row = (ranks, 1, LANES)
    dma = pltpu.SemaphoreType.DMA
    whole = pl.BlockSpec(memory_space=pltpu.VMEM)
    scalars = pl.BlockSpec(memory_space=pltpu.SMEM)
    far = pl.BlockSpec(memory_space=pl.ANY)
    return pl.pallas_call(
        functools.partial(kernel, ranks, shards),
        out_shape=jax.ShapeDtypeStruct((1, ROWS, INNER), BF16),
        in_specs=[far, far, far, whole, whole, scalars, scalars, scalars, whole],
        out_specs=far,
        scratch_shapes=[
            pltpu.VMEM((ROWS, CONV_DIM), BF16),
            pltpu.VMEM((ROWS, INNER), BF16),
            pltpu.VMEM((HEADS, ROWS), BF16),
            pltpu.VMEM((16, CONV_DIM), BF16),
            pltpu.VMEM((16, 1024), F32),
            pltpu.VMEM((16, 1024), BF16),
            pltpu.VMEM((16, 1024), BF16),
            pltpu.VMEM((8, CONV_DIM), F32),
            pltpu.VMEM((8, 384), F32),
            pltpu.VMEM((shards, 8, 384), F32),
            pltpu.VMEM((8, CONV_DIM), F32),
            pltpu.VMEM((1, INNER), F32),
            pltpu.VMEM((2 * ROWS + 16, 2 * LANES), BF16),
            pltpu.VMEM((ROWS, 2 * LANES), BF16),
            pltpu.VMEM((LANES, ROWS), F32),
            pltpu.VMEM((GROUPS, LANES, ROWS), BF16),
            pltpu.VMEM((GROUPS, ROWS, LANES), BF16),
            pltpu.VMEM((GROUPS, ROWS, ROWS), F32),
            pltpu.VMEM(tile, BF16),
            pltpu.VMEM(tile, F32),
            pltpu.VMEM(tile, F32),
            pltpu.VMEM(tile, F32),
            pltpu.VMEM((GROUPS, ROWS, LANES), F32),
            pltpu.VMEM((ROWS, INNER), BF16),
            pltpu.VMEM(pair, BF16),
            pltpu.VMEM(pair, BF16),
            pltpu.VMEM(row, F32),
            pltpu.VMEM(row, F32),
            pltpu.VMEM(pair, BF16),
            pltpu.VMEM(pair, BF16),
            dma((4,)),
            dma((GROUPS,)),
            dma((2,)),
            dma((2,)),
            dma((2,)),
            dma((2,)),
            dma,
            dma((ranks,)),
        ],
        compiler_params=pltpu.CompilerParams(
            collective_id=0, has_side_effects=True, vmem_limit_bytes=40 * 1024 * 1024
        ),
        name="mixer",
    )(*operands)


def solution(mesh):
    ranks, shards = mesh.shape["seq"], mesh.shape["fsdp"]

    def body(conv_input, gate_input, step_input, conv_weight, conv_bias, decay_log, step_bias, skip_weight, norm_gain):
        return mixer(
            ranks, shards, conv_input, gate_input, jnp.swapaxes(step_input, 1, 2),
            conv_weight, conv_bias, decay_log, step_bias, skip_weight, norm_gain,
        )

    return jax.shard_map(
        body,
        mesh=mesh,
        in_specs=(
            P("fsdp", "seq", None),
            P("fsdp", "seq", None),
            P("fsdp", "seq", None),
            P(None, "fsdp"),
            P("fsdp"),
            P("fsdp"),
            P("fsdp"),
            P("fsdp"),
            P("fsdp"),
        ),
        out_specs=P("fsdp", "seq", None),
        check_vma=False,
    )
```

time: 907 us -> 118 us (0.13)
  the two profiles are of different devices: /device:TPU:504 before, /device:TPU:56 now
where the time goes in v1:
time: 118 us; the launch traced here: 116 us
  Pallas kernels  107 us (91%)
  local copies, waits for them, and re-layouts  8.24 us (7%)
    pallas_call x1, Pallas kernels, mixer(): pl.pallas_call(functools.partial(kernel, ranks, shards), out_shape=jax.Sh...  107 us
    unnamed x19, local copies, waits for them, and re-layouts  8.24 us

profile of v1, /device:TPU:56, one launch (start us, length us, event | category | flops | bytes accessed | tf_op | source)
XLA Modules:
  0.0 115.7 jit_solution(17039882240718106696)
XLA Ops:
  0.0 0.0 copy-start
  0.0 1.3 %copy-done = bf16[1,128,5120]{2,1,0:T(8,128)(2,1)S(1)} copy-done((bf16[1,128,5120]{2,1,0:T(8,128)(2,1)S(1)}, bf16[1,128,5120]{2,1,0:T(8,128)(2,1)}, u32[]{:S(2)}) %copy-start) | copy-done | bytes 1310744
  1.3 0.0 copy-start.1
  1.3 1.2 %copy-done.1 = bf16[1,128,4096]{2,1,0:T(8,128)(2,1)S(1)} copy-done((bf16[1,128,4096]{2,1,0:T(8,128)(2,1)S(1)}, bf16[1,128,4096]{2,1,0:T(8,128)(2,1)}, u32[]{:S(2)}) %copy-start.1) | copy-done | bytes 1048600
  2.5 0.0 copy-start.2
  2.5 0.7 copy-done.2
  3.3 0.0 copy-start.3
  3.3 0.7 copy-done.3
  4.0 0.0 copy-start.4
  4.0 0.7 copy-done.4
  4.6 0.0 copy-start.5
  4.6 0.7 copy-done.5
  5.3 0.0 copy-start.6
  5.3 0.7 copy-done.6
  6.0 0.0 copy-start.7
  6.0 0.7 copy-done.7
  6.6 0.0 copy-start.8
  6.6 0.7 copy-done.8
  7.3 107.4 %mixer.1 = bf16[1,128,4096]{2,1,0:T(8,128)(2,1)S(1)} custom-call(bf16[1,128,5120]{2,1,0:T(8,128)(2,1)S(1)} %copy-done, bf16[1,128,4096]{2,1,0:T(8,128)(2,1)S(1)} %copy-done.1, bf16[1,64,128]{2,1,0:T(8,128)(2,1)S(1)} %bitcast.1, f32[4,320]{1,0:T(4,128)S(1)} %copy-done.3, f32[320]{0:T(512)S(1)} %copy-done.4, f32[4]{0:T(128)S(1)} %copy-done.6, f32[4]{0:T(128)S(1)} %copy-done.7, ...), custom_call_target="tpu_custom_call" | custom-call | tf_op jit(solution)/shard_map/mixer/pallas_call | solution.py:314
  114.7 1.0 copy.11
Async XLA Ops:
  0.0 1.3 %copy-start = (bf16[1,128,5120]{2,1,0:T(8,128)(2,1)S(1)}, bf16[1,128,5120]{2,1,0:T(8,128)(2,1)}, u32[]{:S(2)}) copy-start(bf16[1,128,5120]{2,1,0:T(8,128)(2,1)} %conv_hbm.1) | copy-start | bytes 3932164
  1.3 1.2 %copy-start.1 = (bf16[1,128,4096]{2,1,0:T(8,128)(2,1)S(1)}, bf16[1,128,4096]{2,1,0:T(8,128)(2,1)}, u32[]{:S(2)}) copy-start(bf16[1,128,4096]{2,1,0:T(8,128)(2,1)} %gate_hbm.1) | copy-start | bytes 3145732
  2.5 0.7 copy-start.2
  3.3 0.7 copy-start.3
  4.0 0.7 copy-start.4
  4.6 0.7 copy-start.5
  5.3 0.7 copy-start.6
  6.0 0.7 copy-start.7
  6.6 0.7 copy-start.8

commit v2 on v1

--- a/solution.py
+++ b/solution.py
@@ -18,6 +18,18 @@
 TILES = INNER // LANES
 PER_GROUP = TILES // GROUPS
 LOG2E = 1.4426950408889634
+SIDE = 4
+CHUNKS = 4
+OFFSETS = (
+    ((1, 1), (7, 3), (1, 3), (7, 1)),
+    ((2, 1), (6, 3), (2, 3), (6, 1)),
+    ((3, 1), (5, 3), (3, 3), (5, 1)),
+    ((1, 0), (7, 0), (0, 1), (0, 3)),
+    ((2, 0), (6, 0), (0, 2), (4, 0)),
+    ((3, 0), (5, 0), (4, 1), (4, 3)),
+    ((2, 2), (6, 2), (3, 2), (5, 2)),
+    ((1, 2), (7, 2), (4, 2), (0, 0)),
+)
 MESH = pl.DeviceIdType.MESH
 F32 = jnp.float32
 BF16 = jnp.bfloat16
@@ -46,16 +58,40 @@
     )
 
 
+def packed(group):
+    code = 0
+    for along_z, along_y in reversed(group):
+        code = code * 32 + along_z * SIDE + along_y
+    return code
+
+
+def for_groups(step):
+    def one(_, codes):
+        first = codes[0]
+        step([lax.rem(lax.div(first, 32**i), 32) for i in range(4)])
+        return codes[1:] + codes[:1]
+
+    lax.fori_loop(0, len(OFFSETS), one, tuple(jnp.int32(packed(group)) for group in OFFSETS))
+
+
+def shifted(rank, offset, ranks, sign=1):
+    high = ranks // SIDE
+    z = lax.rem(lax.div(rank, SIDE) + high + sign * lax.div(offset, SIDE), high)
+    y = lax.rem(lax.rem(rank, SIDE) + SIDE + sign * lax.rem(offset, SIDE), SIDE)
+    return z * SIDE + y
+
+
 def kernel(
     ranks, shards,
-    conv_hbm, gate_hbm, step_hbm, weight_ref, bias_ref, decay_ref, step_bias_ref, skip_ref, gain_ref,
-    out_hbm,
+    conv_hbm, gate_hbm, step_hbm, weight_hbm, bias_hbm, decay_hbm, step_bias_hbm, skip_hbm, gain_hbm,
+    out_ref,
+    weight_ref, bias_ref, decay_ref, step_bias_ref, skip_ref, gain_ref,
     conv_v, gate_v, step_v, tail_v, halo_pack, halo_send, halo_recv, halo,
     par_send, par, wfull, gfull,
     wide, cparts, logdt, keyt, query, scores,
-    xs, vals, expc, gates, square, out_v,
+    xs, vals, expc, gates, square,
     local_send, local_recv, decay_send, decay_recv, state_send, state_recv,
-    load_sem, out_sem, halo_sem, par_sem, loc_sem, dec_sem, st_send_sem, st_recv_sem,
+    load_sem, halo_sem, par_sem, loc_sem, dec_sem, st_send_sem, st_recv_sem,
 ):
     me = lax.axis_index("seq")
     shard = lax.axis_index("fsdp")
@@ -67,6 +103,15 @@
     step_load = load(step_hbm.at[0], step_v, 1)
     conv_load = load(conv_hbm.at[0], conv_v, 2)
     gate_load = load(gate_hbm.at[0], gate_v, 3)
+    small_loads = [
+        load(src, dst, 4 + i)
+        for i, (src, dst) in enumerate((
+            (weight_hbm, weight_ref), (bias_hbm, bias_ref), (gain_hbm, gain_ref),
+            (decay_hbm, decay_ref), (step_bias_hbm, step_bias_ref), (skip_hbm, skip_ref),
+        ))
+    ]
+    for small_load in small_loads:
+        small_load.start()
     tail_load.start()
     step_load.start()
     conv_load.start()
@@ -88,6 +133,8 @@
     width = CONV_DIM // shards
     heads = HEADS // shards
     par_send[...] = jnp.zeros_like(par_send)
+    for small_load in small_loads:
+        small_load.wait()
     odd = lax.rem(shard, 2)
 
     @pl.when(odd == 0)
@@ -211,18 +258,34 @@
         xs[o] = x.astype(BF16)
         vals[o] = x * spread[2 * ROWS : 2 * ROWS + 1]
         weighted = (x * spread[0:ROWS]).astype(BF16)
-        state_ref[...] = dot(keyt[o // PER_GROUP], weighted).astype(BF16)
+        state_ref[...] = dot(keyt[lax.div(o, PER_GROUP)], weighted).astype(BF16)
         decay_out[...] = spread[2 * ROWS - 1 : 2 * ROWS]
 
-    def first_pass(k, c):
-        o = lax.rem(me + k, ranks)
-        local_state(o, local_send.at[o], decay_send.at[o])
-        remote(local_send.at[o], local_recv.at[me], loc_sem.at[0], loc_sem.at[1], {"seq": o}).start()
-        remote(decay_send.at[o], decay_recv.at[me], dec_sem.at[0], dec_sem.at[1], {"seq": o}).start()
-        return c
-
-    lax.fori_loop(1, ranks, first_pass, 0)
-    local_state(me, local_recv.at[me], decay_recv.at[me])
+    tall = LANES // CHUNKS
+
+    def send_tiles(targets, offsets, src, dst, send_sem, recv_sem):
+        for c in range(CHUNKS):
+            for target, offset in zip(targets, offsets):
+
+                @pl.when(offset != 0)
+                def _():
+                    rows = pl.ds(c * tall, tall)
+                    remote(src.at[target, rows], dst.at[me, rows], send_sem, recv_sem, {"seq": target}).start()
+
+    def first_pass(offsets):
+        targets = [shifted(me, offset, ranks) for offset in offsets]
+        for target, offset in zip(targets, offsets):
+            local_state(target, local_send.at[target], decay_send.at[target])
+
+            @pl.when(offset != 0)
+            def _():
+                remote(decay_send.at[target], decay_recv.at[me], dec_sem.at[0], dec_sem.at[1], {"seq": target}).start()
+
+        send_tiles(targets, offsets, local_send, local_recv, loc_sem.at[0], loc_sem.at[1])
+
+    for_groups(first_pass)
+    local_recv[me] = local_send[me]
+    decay_recv[me] = decay_send[me]
 
     ones_row = lax.rem(lax.broadcasted_iota(jnp.int32, (2 * LANES, 2 * LANES), 0), HEADS)
     ones_half = lax.broadcasted_iota(jnp.int32, (2 * LANES, 2 * LANES), 1) // LANES
@@ -230,7 +293,7 @@
     def inside(o, c):
         pick = jnp.where(ones_row == ones_half + 2 * o, 1.0, 0.0).astype(BF16)
         spread = dot(cparts[...], pick)
-        score = scores[o // PER_GROUP]
+        score = scores[lax.div(o, PER_GROUP)]
         x = xs[o]
         zero = jnp.zeros_like(x)
         total = vals[o]
@@ -255,52 +318,44 @@
 
     lax.fori_loop(0, ranks, carry, jnp.zeros((LANES, LANES), F32))
 
-    def send_state(k, c):
-        s = lax.rem(me + k, ranks)
-        remote(state_send.at[s], state_recv.at[me], st_send_sem, st_recv_sem.at[me], {"seq": s}).start()
-        return c
-
-    lax.fori_loop(1, ranks, send_state, 0)
+    def second_pass(offsets):
+        targets = [shifted(me, offset, ranks) for offset in offsets]
+        send_tiles(targets, offsets, state_send, state_recv, st_send_sem, st_recv_sem.at[me])
+
+    for_groups(second_pass)
+    state_recv[me] = state_send[me]
     square[...] = jnp.zeros_like(square)
 
-    def finish(o, state):
-        g = o // PER_GROUP
-        value = (vals[o] + dot(query[g], state) * expc[o]) * gates[o].astype(F32)
-        vals[o] = value
-        square[g] = square[g] + value * value
-
-    finish(me, state_send[me])
-
-    def arrive(k, c):
-        o = lax.rem(me + ranks - k, ranks)
-        slot = state_recv.at[o]
-        pltpu.make_async_copy(slot, slot, st_recv_sem.at[o]).wait()
-        finish(o, state_recv[o])
-        return c
-
-    lax.fori_loop(1, ranks, arrive, 0)
-
-    writes = []
+    def arrive(offsets):
+        for offset in offsets:
+            o = shifted(me, offset, ranks, -1)
+
+            @pl.when(offset != 0)
+            def _():
+                slot = state_recv.at[o]
+                pltpu.make_async_copy(slot, slot, st_recv_sem.at[o]).wait()
+
+            g = lax.div(o, PER_GROUP)
+            value = (vals[o] + dot(query[g], state_recv[o]) * expc[o]) * gates[o].astype(F32)
+            vals[o] = value
+            square[g] = square[g] + value * value
+
+    for_groups(arrive)
+
     for g in range(GROUPS):
         mean = jnp.sum(square[g], axis=1, keepdims=True) * (1.0 / (PER_GROUP * LANES))
         inverse = lax.rsqrt(mean + EPS)
         for j in range(PER_GROUP):
             o = g * PER_GROUP + j
-            out_v[:, o * LANES : (o + 1) * LANES] = (
+            out_ref[0, :, o * LANES : (o + 1) * LANES] = (
                 vals[o] * inverse * gfull[:, o * LANES : (o + 1) * LANES]
             ).astype(BF16)
-        part = slice(g * 1024, (g + 1) * 1024)
-        write = pltpu.make_async_copy(out_v.at[:, part], out_hbm.at[0, :, part], out_sem.at[g])
-        write.start()
-        writes.append(write)
 
     pltpu.make_async_copy(several, several, par_sem.at[0]).wait()
     pltpu.make_async_copy(most, most, loc_sem.at[0]).wait()
     pltpu.make_async_copy(most_decay, most_decay, dec_sem.at[0]).wait()
     sent = state_send.at[pl.ds(0, ranks - 1)]
     pltpu.make_async_copy(sent, sent, st_send_sem).wait()
-    for write in writes:
-        write.wait()
 
 
 def mixer(ranks, shards, *operands):
@@ -308,15 +363,19 @@
     pair = (ranks, LANES, LANES)
     row = (ranks, 1, LANES)
     dma = pltpu.SemaphoreType.DMA
-    whole = pl.BlockSpec(memory_space=pltpu.VMEM)
-    scalars = pl.BlockSpec(memory_space=pltpu.SMEM)
     far = pl.BlockSpec(memory_space=pl.ANY)
     return pl.pallas_call(
         functools.partial(kernel, ranks, shards),
-        out_shape=jax.ShapeDtypeStruct((1, ROWS, INNER), BF16),
-        in_specs=[far, far, far, whole, whole, scalars, scalars, scalars, whole],
-        out_specs=far,
+        out_shape=pltpu.VMEM((1, ROWS, INNER), BF16),
+        in_specs=[far] * 9,
+        out_specs=pl.BlockSpec(memory_space=pltpu.VMEM),
         scratch_shapes=[
+            pltpu.VMEM((KERNEL, CONV_DIM // shards), F32),
+            pltpu.VMEM((CONV_DIM // shards,), F32),
+            pltpu.SMEM((HEADS // shards,), F32),
+            pltpu.SMEM((HEADS // shards,), F32),
+            pltpu.SMEM((HEADS // shards,), F32),
+            pltpu.VMEM((INNER // shards,), F32),
             pltpu.VMEM((ROWS, CONV_DIM), BF16),
             pltpu.VMEM((ROWS, INNER), BF16),
             pltpu.VMEM((HEADS, ROWS), BF16),
@@ -340,15 +399,13 @@
             pltpu.VMEM(tile, F32),
             pltpu.VMEM(tile, F32),
             pltpu.VMEM((GROUPS, ROWS, LANES), F32),
-            pltpu.VMEM((ROWS, INNER), BF16),
             pltpu.VMEM(pair, BF16),
             pltpu.VMEM(pair, BF16),
             pltpu.VMEM(row, F32),
             pltpu.VMEM(row, F32),
             pltpu.VMEM(pair, BF16),
             pltpu.VMEM(pair, BF16),
-            dma((4,)),
-            dma((GROUPS,)),
+            dma((10,)),
             dma((2,)),
             dma((2,)),
             dma((2,)),
@@ -357,7 +414,7 @@
             dma((ranks,)),
         ],
         compiler_params=pltpu.CompilerParams(
-            collective_id=0, has_side_effects=True, vmem_limit_bytes=40 * 1024 * 1024
+            collective_id=0, has_side_effects=True, vmem_limit_bytes=60 * 1024 * 1024
         ),
         name="mixer",
     )(*operands)

time: 118 us -> 90.2 us (0.76)
  the two profiles are of different devices: /device:TPU:56 before, /device:TPU:48 now
where the time goes in v2:
time: 90.2 us; the launch traced here: 90.1 us
  Pallas kernels  89.1 us (99%)
  local copies, waits for them, and re-layouts  0.97 us (1%)
    pallas_call x1, Pallas kernels, mixer(): pl.pallas_call(functools.partial(kernel, ranks, shards), out_shape=pltpu....  89.1 us

profile of v2, /device:TPU:48, one launch (start us, length us, event | category | flops | bytes accessed | tf_op | source)
XLA Modules:
  0.0 90.1 jit_solution(7541123047716743601)
XLA Ops:
  0.0 89.1 %mixer.1 = bf16[1,128,4096]{2,1,0:T(8,128)(2,1)S(1)} custom-call(bf16[1,128,5120]{2,1,0:T(8,128)(2,1)} %conv_hbm.1, bf16[1,128,4096]{2,1,0:T(8,128)(2,1)} %gate_hbm.1, bf16[1,64,128]{2,1,0:T(8,128)(2,1)} %bitcast.1, f32[4,320]{1,0:T(4,128)} %weight_hbm.1, f32[320]{0:T(512)} %bias_hbm.1, f32[4]{0:T(128)} %decay_hbm.1, f32[4]{0:T(128)} %step_bias_hbm.1, ...), custom_call_target="tpu_custom_call" | custom-call | tf_op jit(solution)/shard_map/mixer/pallas_call | solution.py:367
  89.1 1.0 %copy.11 = bf16[1,128,4096]{2,1,0:T(8,128)(2,1)} copy(bf16[1,128,4096]{2,1,0:T(8,128)(2,1)S(1)} %mixer.1) | data formatting | bytes 2097152

commit v3 on v2

--- a/solution.py
+++ b/solution.py
@@ -18,17 +18,19 @@
 TILES = INNER // LANES
 PER_GROUP = TILES // GROUPS
 LOG2E = 1.4426950408889634
+INSIDE_FIRST = 12
 SIDE = 4
+PIECES = 2
 CHUNKS = 4
 OFFSETS = (
-    ((1, 1), (7, 3), (1, 3), (7, 1)),
+    ((3, 0), (5, 0), (1, 2), (7, 2)),
     ((2, 1), (6, 3), (2, 3), (6, 1)),
-    ((3, 1), (5, 3), (3, 3), (5, 1)),
-    ((1, 0), (7, 0), (0, 1), (0, 3)),
-    ((2, 0), (6, 0), (0, 2), (4, 0)),
-    ((3, 0), (5, 0), (4, 1), (4, 3)),
-    ((2, 2), (6, 2), (3, 2), (5, 2)),
-    ((1, 2), (7, 2), (4, 2), (0, 0)),
+    ((2, 0), (6, 0), (2, 2), (6, 2)),
+    ((1, 1), (7, 3), (3, 3), (5, 1)),
+    ((1, 0), (7, 0), (3, 2), (5, 2)),
+    ((1, 3), (7, 1), (3, 1), (5, 3)),
+    ((0, 1), (0, 3), (4, 0), (4, 2)),
+    ((4, 1), (4, 3), (0, 2), (0, 0)),
 )
 MESH = pl.DeviceIdType.MESH
 F32 = jnp.float32
@@ -91,7 +93,7 @@
     wide, cparts, logdt, keyt, query, scores,
     xs, vals, expc, gates, square,
     local_send, local_recv, decay_send, decay_recv, state_send, state_recv,
-    load_sem, halo_sem, par_sem, loc_sem, dec_sem, st_send_sem, st_recv_sem,
+    load_sem, ready, halo_sem, par_sem, loc_sem, dec_sem, st_send_sem, st_recv_sem,
 ):
     me = lax.axis_index("seq")
     shard = lax.axis_index("fsdp")
@@ -119,16 +121,18 @@
 
     barrier = pltpu.get_barrier_semaphore()
 
-    def greet_rank(k, c):
-        pl.semaphore_signal(barrier, inc=1, device_id={"seq": lax.rem(me + k, ranks)}, device_id_type=MESH)
-        return c
-
     def greet_shard(k, c):
         pl.semaphore_signal(barrier, inc=1, device_id={"fsdp": lax.rem(shard + k, shards)}, device_id_type=MESH)
         return c
 
+    def greet_rank(offset, c):
+        pl.semaphore_signal(barrier, inc=1, device_id={"seq": shifted(me, offset, ranks)}, device_id_type=MESH)
+        return c
+
+    high = ranks // SIDE
     lax.fori_loop(1, shards, greet_shard, 0)
-    lax.fori_loop(1, ranks, greet_rank, 0)
+    lax.fori_loop(1, SIDE, greet_rank, 0)
+    lax.fori_loop(1, high, lambda k, c: greet_rank(k * SIDE, c), 0)
 
     width = CONV_DIM // shards
     heads = HEADS // shards
@@ -164,17 +168,23 @@
             halo_pack[r * 5 + c : r * 5 + c + 1, :] = tail[13 + r : 14 + r, c * 1024 : (c + 1) * 1024]
     halo_send[...] = halo_pack[...].astype(BF16)
 
-    pl.semaphore_wait(barrier, ranks + shards - 2)
-
-    halo_copy = remote(halo_send, halo_recv, halo_sem.at[0], halo_sem.at[1], {"seq": lax.rem(me + 1, ranks)})
-    halo_copy.start()
+    pl.semaphore_wait(barrier, shards - 1 + SIDE - 1 + high - 1)
 
     def send_par(k, c):
         remote(par_send, par.at[shard], par_sem.at[0], par_sem.at[1],
                {"fsdp": lax.rem(shard + k, shards)}).start()
         return c
 
+    def tell(offset, c):
+        pl.semaphore_signal(ready, inc=1, device_id={"seq": shifted(me, offset, ranks)}, device_id_type=MESH)
+        return c
+
+    lax.fori_loop(1, SIDE, tell, 0)
     lax.fori_loop(1, shards, send_par, 0)
+    pl.semaphore_wait(ready, SIDE - 1)
+    halo_copy = remote(halo_send, halo_recv, halo_sem.at[0], halo_sem.at[1], {"seq": lax.rem(me + 1, ranks)})
+    halo_copy.start()
+
     par[shard] = par_send[...]
 
     gate_load.wait()
@@ -261,15 +271,16 @@
         state_ref[...] = dot(keyt[lax.div(o, PER_GROUP)], weighted).astype(BF16)
         decay_out[...] = spread[2 * ROWS - 1 : 2 * ROWS]
 
-    tall = LANES // CHUNKS
-
-    def send_tiles(targets, offsets, src, dst, send_sem, recv_sem):
+    part = LANES // PIECES
+    tall = part // CHUNKS
+
+    def send_tiles(piece, targets, offsets, src, dst, send_sem, recv_sem):
         for c in range(CHUNKS):
             for target, offset in zip(targets, offsets):
 
                 @pl.when(offset != 0)
                 def _():
-                    rows = pl.ds(c * tall, tall)
+                    rows = pl.ds(piece * part + c * tall, tall)
                     remote(src.at[target, rows], dst.at[me, rows], send_sem, recv_sem, {"seq": target}).start()
 
     def first_pass(offsets):
@@ -281,9 +292,14 @@
             def _():
                 remote(decay_send.at[target], decay_recv.at[me], dec_sem.at[0], dec_sem.at[1], {"seq": target}).start()
 
-        send_tiles(targets, offsets, local_send, local_recv, loc_sem.at[0], loc_sem.at[1])
+        send_local(0, targets, offsets)
+
+    def send_local(piece, targets, offsets):
+        send_tiles(piece, targets, offsets, local_send, local_recv, loc_sem.at[PIECES], loc_sem.at[piece])
 
     for_groups(first_pass)
+    for piece in range(1, PIECES):
+        for_groups(lambda offsets: send_local(piece, [shifted(me, offset, ranks) for offset in offsets], offsets))
     local_recv[me] = local_send[me]
     decay_recv[me] = decay_send[me]
 
@@ -305,24 +321,31 @@
         vals[o] = total
         return c
 
-    lax.fori_loop(0, TILES, inside, 0)
+    def send_states(piece):
+        here = slice(piece * part, (piece + 1) * part)
+        landed = local_recv.at[pl.ds(0, ranks - 1), here]
+        pltpu.make_async_copy(landed, landed, loc_sem.at[piece]).wait()
+
+        def carry(s, state):
+            state_send[s, here] = state.astype(BF16)
+            return state * decay_recv[s] + local_recv[s, here].astype(F32)
+
+        lax.fori_loop(0, ranks, carry, jnp.zeros((part, LANES), F32), unroll=4)
+
+        def second_pass(offsets):
+            targets = [shifted(me, offset, ranks) for offset in offsets]
+            send_tiles(piece, targets, offsets, state_send, state_recv, st_send_sem, st_recv_sem.at[me])
+
+        for_groups(second_pass)
 
     most = local_recv.at[pl.ds(0, ranks - 1)]
-    pltpu.make_async_copy(most, most, loc_sem.at[1]).wait()
     most_decay = decay_recv.at[pl.ds(0, ranks - 1)]
+    lax.fori_loop(0, INSIDE_FIRST, inside, 0)
     pltpu.make_async_copy(most_decay, most_decay, dec_sem.at[1]).wait()
-
-    def carry(s, state):
-        state_send[s] = state.astype(BF16)
-        return state * decay_recv[s] + local_recv[s].astype(F32)
-
-    lax.fori_loop(0, ranks, carry, jnp.zeros((LANES, LANES), F32))
-
-    def second_pass(offsets):
-        targets = [shifted(me, offset, ranks) for offset in offsets]
-        send_tiles(targets, offsets, state_send, state_recv, st_send_sem, st_recv_sem.at[me])
-
-    for_groups(second_pass)
+    send_states(0)
+    lax.fori_loop(INSIDE_FIRST, TILES, inside, 0)
+    for piece in range(1, PIECES):
+        send_states(piece)
     state_recv[me] = state_send[me]
     square[...] = jnp.zeros_like(square)
 
@@ -352,7 +375,7 @@
             ).astype(BF16)
 
     pltpu.make_async_copy(several, several, par_sem.at[0]).wait()
-    pltpu.make_async_copy(most, most, loc_sem.at[0]).wait()
+    pltpu.make_async_copy(most, most, loc_sem.at[PIECES]).wait()
     pltpu.make_async_copy(most_decay, most_decay, dec_sem.at[0]).wait()
     sent = state_send.at[pl.ds(0, ranks - 1)]
     pltpu.make_async_copy(sent, sent, st_send_sem).wait()
@@ -406,9 +429,10 @@
             pltpu.VMEM(pair, BF16),
             pltpu.VMEM(pair, BF16),
             dma((10,)),
+            pltpu.SemaphoreType.REGULAR,
             dma((2,)),
             dma((2,)),
-            dma((2,)),
+            dma((PIECES + 1,)),
             dma((2,)),
             dma,
             dma((ranks,)),

time: 90.2 us -> 76.1 us (0.84)
  the two profiles are of different devices: /device:TPU:48 before, /device:TPU:1 now
where the time goes in v3:
time: 76.1 us; the launch traced here: 75.9 us
  Pallas kernels  74.9 us (98%)
  local copies, waits for them, and re-layouts  0.97 us (1%)
    pallas_call x1, Pallas kernels, mixer(): pl.pallas_call(functools.partial(kernel, ranks, shards), out_shape=pltpu....  74.9 us

profile of v3, /device:TPU:1, one launch (start us, length us, event | category | flops | bytes accessed | tf_op | source)
XLA Modules:
  0.0 75.9 jit_solution(4729490709938644338)
XLA Ops:
  0.0 74.9 %mixer.1 = bf16[1,128,4096]{2,1,0:T(8,128)(2,1)S(1)} custom-call(bf16[1,128,5120]{2,1,0:T(8,128)(2,1)} %conv_hbm.1, bf16[1,128,4096]{2,1,0:T(8,128)(2,1)} %gate_hbm.1, bf16[1,64,128]{2,1,0:T(8,128)(2,1)} %bitcast.1, f32[4,320]{1,0:T(4,128)} %weight_hbm.1, f32[320]{0:T(512)} %bias_hbm.1, f32[4]{0:T(128)} %decay_hbm.1, f32[4]{0:T(128)} %step_bias_hbm.1, ...), custom_call_target="tpu_custom_call" | custom-call | tf_op jit(solution)/shard_map/mixer/pallas_call | solution.py:390
  75.0 1.0 %copy.11 = bf16[1,128,4096]{2,1,0:T(8,128)(2,1)} copy(bf16[1,128,4096]{2,1,0:T(8,128)(2,1)S(1)} %mixer.1) | data formatting | bytes 2097152

commit v4 on v3

--- a/solution.py
+++ b/solution.py
@@ -121,8 +121,18 @@
 
     barrier = pltpu.get_barrier_semaphore()
 
+    beside = shifted(me, 1, ranks, 1)
+    behind = shifted(me, 1, ranks, -1)
+    own_low = lax.rem(lax.div(shard, 2), 2)
+
+    def peer(k):
+        other = lax.rem(shard + k, shards)
+        return other, lax.rem(lax.div(other, 2), 2) - own_low
+
     def greet_shard(k, c):
-        pl.semaphore_signal(barrier, inc=1, device_id={"fsdp": lax.rem(shard + k, shards)}, device_id_type=MESH)
+        other, rise = peer(k)
+        source = jnp.where(rise == -1, beside, me)
+        pl.semaphore_signal(barrier, inc=1, device_id={"fsdp": other, "seq": source}, device_id_type=MESH)
         return c
 
     def greet_rank(offset, c):
@@ -133,6 +143,17 @@
     lax.fori_loop(1, shards, greet_shard, 0)
     lax.fori_loop(1, SIDE, greet_rank, 0)
     lax.fori_loop(1, high, lambda k, c: greet_rank(k * SIDE, c), 0)
+
+    along_y = lax.rem(me, SIDE)
+
+    @pl.when(along_y == SIDE - 1)
+    def _():
+        greet_rank(SIDE + 1, 0)
+
+    @pl.when(along_y == 0)
+    def _():
+        greet_rank((high - 1) * SIDE + SIDE - 1, 0)
+
 
     width = CONV_DIM // shards
     heads = HEADS // shards
@@ -168,22 +189,32 @@
             halo_pack[r * 5 + c : r * 5 + c + 1, :] = tail[13 + r : 14 + r, c * 1024 : (c + 1) * 1024]
     halo_send[...] = halo_pack[...].astype(BF16)
 
-    pl.semaphore_wait(barrier, shards - 1 + SIDE - 1 + high - 1)
+    peers = shards - 1 + SIDE - 1 + high - 1
+    at_end = jnp.logical_or(along_y == 0, along_y == SIDE - 1)
+
+    @pl.when(at_end)
+    def _():
+        pl.semaphore_wait(barrier, peers + 1)
+
+    @pl.when(jnp.logical_not(at_end))
+    def _():
+        pl.semaphore_wait(barrier, peers)
+
 
     def send_par(k, c):
-        remote(par_send, par.at[shard], par_sem.at[0], par_sem.at[1],
-               {"fsdp": lax.rem(shard + k, shards)}).start()
+        other, rise = peer(k)
+        target = jnp.where(rise == 1, behind, me)
+        remote(par_send, par.at[shard], par_sem.at[0], par_sem.at[1], {"fsdp": other, "seq": target}).start()
         return c
 
     def tell(offset, c):
         pl.semaphore_signal(ready, inc=1, device_id={"seq": shifted(me, offset, ranks)}, device_id_type=MESH)
         return c
 
-    lax.fori_loop(1, SIDE, tell, 0)
     lax.fori_loop(1, shards, send_par, 0)
-    pl.semaphore_wait(ready, SIDE - 1)
     halo_copy = remote(halo_send, halo_recv, halo_sem.at[0], halo_sem.at[1], {"seq": lax.rem(me + 1, ranks)})
     halo_copy.start()
+    lax.fori_loop(1, SIDE, tell, 0)
 
     par[shard] = par_send[...]
 
@@ -274,11 +305,11 @@
     part = LANES // PIECES
     tall = part // CHUNKS
 
-    def send_tiles(piece, targets, offsets, src, dst, send_sem, recv_sem):
+    def send_tiles(piece, targets, wanted, src, dst, send_sem, recv_sem):
         for c in range(CHUNKS):
-            for target, offset in zip(targets, offsets):
-
-                @pl.when(offset != 0)
+            for target, want in zip(targets, wanted):
+
+                @pl.when(want)
                 def _():
                     rows = pl.ds(piece * part + c * tall, tall)
                     remote(src.at[target, rows], dst.at[me, rows], send_sem, recv_sem, {"seq": target}).start()
@@ -292,11 +323,15 @@
             def _():
                 remote(decay_send.at[target], decay_recv.at[me], dec_sem.at[0], dec_sem.at[1], {"seq": target}).start()
 
-        send_local(0, targets, offsets)
+            send_local(0, [target], [offset])
+
+    last = ranks - 1
 
     def send_local(piece, targets, offsets):
-        send_tiles(piece, targets, offsets, local_send, local_recv, loc_sem.at[PIECES], loc_sem.at[piece])
-
+        wanted = [jnp.logical_and(offset != 0, me != last) for offset in offsets]
+        send_tiles(piece, targets, wanted, local_send, local_recv, loc_sem.at[PIECES], loc_sem.at[piece])
+
+    pl.semaphore_wait(ready, SIDE - 1)
     for_groups(first_pass)
     for piece in range(1, PIECES):
         for_groups(lambda offsets: send_local(piece, [shifted(me, offset, ranks) for offset in offsets], offsets))
@@ -321,10 +356,17 @@
         vals[o] = total
         return c
 
+    def wait_either(first, view, sem, one, other):
+        for chosen, n in ((first, one), (jnp.logical_not(first), other)):
+            if n:
+
+                @pl.when(chosen)
+                def _():
+                    pltpu.make_async_copy(view(n), view(n), sem).wait()
+
     def send_states(piece):
         here = slice(piece * part, (piece + 1) * part)
-        landed = local_recv.at[pl.ds(0, ranks - 1), here]
-        pltpu.make_async_copy(landed, landed, loc_sem.at[piece]).wait()
+        wait_either(me == last, lambda n: local_recv.at[pl.ds(0, n), here], loc_sem.at[piece], last, last - 1)
 
         def carry(s, state):
             state_send[s, here] = state.astype(BF16)
@@ -334,11 +376,11 @@
 
         def second_pass(offsets):
             targets = [shifted(me, offset, ranks) for offset in offsets]
-            send_tiles(piece, targets, offsets, state_send, state_recv, st_send_sem, st_recv_sem.at[me])
+            wanted = [jnp.logical_and(offset != 0, target != 0) for target, offset in zip(targets, offsets)]
+            send_tiles(piece, targets, wanted, state_send, state_recv, st_send_sem, st_recv_sem.at[me])
 
         for_groups(second_pass)
 
-    most = local_recv.at[pl.ds(0, ranks - 1)]
     most_decay = decay_recv.at[pl.ds(0, ranks - 1)]
     lax.fori_loop(0, INSIDE_FIRST, inside, 0)
     pltpu.make_async_copy(most_decay, most_decay, dec_sem.at[1]).wait()
@@ -353,7 +395,7 @@
         for offset in offsets:
             o = shifted(me, offset, ranks, -1)
 
-            @pl.when(offset != 0)
+            @pl.when(jnp.logical_and(offset != 0, me != 0))
             def _():
                 slot = state_recv.at[o]
                 pltpu.make_async_copy(slot, slot, st_recv_sem.at[o]).wait()
@@ -362,6 +404,10 @@
             value = (vals[o] + dot(query[g], state_recv[o]) * expc[o]) * gates[o].astype(F32)
             vals[o] = value
             square[g] = square[g] + value * value
+
+    @pl.when(me == 0)
+    def _():
+        state_recv[...] = jnp.zeros_like(state_recv)
 
     for_groups(arrive)
 
@@ -375,10 +421,9 @@
             ).astype(BF16)
 
     pltpu.make_async_copy(several, several, par_sem.at[0]).wait()
-    pltpu.make_async_copy(most, most, loc_sem.at[PIECES]).wait()
+    wait_either(me == last, lambda n: local_recv.at[pl.ds(0, n)], loc_sem.at[PIECES], 0, last)
     pltpu.make_async_copy(most_decay, most_decay, dec_sem.at[0]).wait()
-    sent = state_send.at[pl.ds(0, ranks - 1)]
-    pltpu.make_async_copy(sent, sent, st_send_sem).wait()
+    wait_either(me == 0, lambda n: state_send.at[pl.ds(0, n)], st_send_sem, last, last - 1)
 
 
 def mixer(ranks, shards, *operands):

time: 76.1 us -> 77.5 us (1.018)
  the two profiles are of different devices: /device:TPU:1 before, /device:TPU:56 now
where the time goes in v4:
time: 77.5 us; the launch traced here: 77.4 us
  Pallas kernels  76.4 us (99%)
  local copies, waits for them, and re-layouts  0.97 us (1%)
    pallas_call x1, Pallas kernels, mixer(): pl.pallas_call(functools.partial(kernel, ranks, shards), out_shape=pltpu....  76.4 us

profile of v4, /device:TPU:56, one launch (start us, length us, event | category | flops | bytes accessed | tf_op | source)
XLA Modules:
  0.0 77.4 jit_solution(15305230885216909624)
XLA Ops:
  0.0 76.4 %mixer.1 = bf16[1,128,4096]{2,1,0:T(8,128)(2,1)S(1)} custom-call(bf16[1,128,5120]{2,1,0:T(8,128)(2,1)} %conv_hbm.1, bf16[1,128,4096]{2,1,0:T(8,128)(2,1)} %gate_hbm.1, bf16[1,64,128]{2,1,0:T(8,128)(2,1)} %bitcast.1, f32[4,320]{1,0:T(4,128)} %weight_hbm.1, f32[320]{0:T(512)} %bias_hbm.1, f32[4]{0:T(128)} %decay_hbm.1, f32[4]{0:T(128)} %step_bias_hbm.1, ...), custom_call_target="tpu_custom_call" | custom-call | tf_op jit(solution)/shard_map/mixer/pallas_call | solution.py:435
  76.4 1.0 %copy.11 = bf16[1,128,4096]{2,1,0:T(8,128)(2,1)} copy(bf16[1,128,4096]{2,1,0:T(8,128)(2,1)S(1)} %mixer.1) | data formatting | bytes 2097152
